TPU v7x, 32 devices: a whole 2x2x4 slice. The times are simulated.
32 devices in a mesh: req: 8 (over z, y), head: 4 (over x, core).
Axes of the slice: x: 2, y: 2, z: 4, core: 2. Of those that a mesh axis runs over, the one named last changes fastest.
Arguments:
- tokens: bfloat16 [512, 1024], P(('req', 'head')), may hold values from -6 to 6
- gains: float32 [2, 1024], replicated, may hold values from 0.1 to 1.9
- qkv_weight: bfloat16 [3, 1024, 1024], P(None, None, 'head'), may hold values from -0.1875 to 0.1875
- out_weight: bfloat16 [1024, 1024], replicated, may hold values from -0.1875 to 0.1875
- gate_up_weight: bfloat16 [2, 1024, 4096], P(None, None, 'head'), may hold values from -0.1875 to 0.1875
- down_weight: bfloat16 [4096, 1024], P('head'), may hold values from -0.09375 to 0.09375
- variate_bias: float32 [2, 16], replicated, may hold values from -4 to 4
- page_cache: bfloat16 [2, 160, 128, 1024], P(None, 'req', None, 'head'), may hold values from -210 to 210
- page_variates: int32 [160, 128], P('req'), may hold values from 0 to 3
- token_variates: int32 [512], replicated, may hold values from 0 to 3
- cache_len: int32 [8], replicated, may hold values from 64 to 4096, as said below
- page_table: int32 [8, 32], replicated, may hold values from -1 to 159, as said below
- parents: int32 [8, 64], P('req'), may hold values from -1 to 55, as said below
- accepted: int32 [8, 8], P('req'), may hold values from -1 to 63, as said below
Outputs:
- mixed: bfloat16 [512, 1024], P(('req', 'head'))
- attended: bfloat16 [512, 1024], P('req', 'head')
- new_kv: bfloat16 [2, 8, 8, 1024], P(None, 'req', None, 'head')
Inputs may be any that keep to these rules, and one draw needn't show every extreme that they name: `cache_len`: exactly half of the requests have 128 // 2 to 128 cached positions, the others 4096 // 2 + 1 to 4096. `page_table`: entry [r, b] is the page holding request r's positions b * 128 to b * 128 + 127 for b below ceil(cache_len[r] / 128), and -1 from there on; no page is listed twice. `parents`: node i lies on level i // 8; nodes of level 0 have parent -1, every other node's parent lies on the level before. `accepted`: row r lists a path of request r's tree from a level-0 node downward, one node a level, then -1; its length is 1 to 8, and 8 in some row.
All inputs are finite; a program needn't handle non-finite values.
Results may differ from a plain program's by a relative error of at most 0.015.
The roundings to bfloat16 on the way count: a program that leaves them out, or rounds other values in their place, can miss the bound.
Values may be sent and summed in bfloat16 or wider, within the bound.
A program may use at most 192 MiB of HBM per device.

v0:
```python
import math

import jax
import jax.numpy as jnp
from jax import lax
from jax.sharding import PartitionSpec as P

HD = 64
LEVELS = 8


epsilon = 1e-06
masked_score = -1e30
highest = lax.Precision.HIGHEST


def rms_scaled(rows, gain):
    values = rows.astype(jnp.float32)
    return values * lax.rsqrt(jnp.mean(values * values, axis=-1, keepdims=True) + epsilon) * gain


def merge_parts(first, second):
    max_one, total_one, out_one = first
    max_two, total_two, out_two = second
    highest_max = jnp.maximum(max_one, max_two)
    factor_one = jnp.exp(max_one - highest_max)
    factor_two = jnp.exp(max_two - highest_max)
    return (
        highest_max,
        total_one * factor_one + total_two * factor_two,
        out_one * factor_one[..., None] + out_two * factor_two[..., None],
    )


def shards(
    tokens,
    gains,
    qkv_weight,
    out_weight,
    gate_up_weight,
    down_weight,
    variate_bias,
    page_cache,
    page_variates,
    token_variates,
    cache_len,
    page_table,
    parents,
    accepted,
):
    scale = 1.0 / math.sqrt(HD)
    local_req, tree = parents.shape
    pool, page = page_variates.shape
    requests = cache_len.shape[0]
    qdl = qkv_weight.shape[2]
    head_local = qdl // HD
    head_slot = lax.axis_index("head")
    req_slot = lax.axis_index("req")
    bias_local = lax.dynamic_slice_in_dim(variate_bias, head_slot * head_local, head_local, 1)
    same_bias = bias_local[0]
    other_bias = bias_local[1]
    normed = rms_scaled(tokens, gains[0]).astype(jnp.bfloat16)
    projected = jnp.einsum(
        "td,cdq->ctq",
        lax.all_gather(normed, "head", axis=0, tiled=True),
        qkv_weight,
        preferred_element_type=jnp.float32,
    ).astype(jnp.bfloat16)
    query = projected[0]
    key_new = projected[1]
    value_new = projected[2]
    all_queries = lax.all_gather(query, "req", axis=0, tiled=True)
    global_ids = req_slot * pool + jnp.arange(pool, dtype=jnp.int32)
    matching = (page_table[:, :, None] == global_ids[None, None, :]).astype(jnp.int32)
    owner = jnp.sum(matching * jnp.arange(requests, dtype=jnp.int32)[:, None, None], axis=(0, 1))
    page_order = jnp.sum(
        matching * jnp.arange(page_table.shape[1], dtype=jnp.int32)[None, :, None], axis=(0, 1)
    )
    owner_len = jnp.sum(matching * cache_len[:, None, None], axis=(0, 1))
    in_use = jnp.sum(matching, axis=(0, 1))
    filled = jnp.clip(owner_len - page_order * page, 0, page) * in_use
    valid = jnp.arange(page, dtype=jnp.int32)[None, :] < filled[:, None]
    page_queries = jnp.take(all_queries.reshape(requests, tree, head_local, HD), owner, axis=0)
    query_variates = jnp.take(token_variates.reshape(requests, tree), owner, axis=0)
    cache_keys = page_cache[0].reshape(pool, page, head_local, HD)
    cache_values = page_cache[1].reshape(pool, page, head_local, HD)
    scores = (
        jnp.einsum("pthd,pkhd->pthk", page_queries, cache_keys, preferred_element_type=jnp.float32)
        * scale
    )
    same_page = query_variates[:, :, None] == page_variates[:, None, :]
    scores = scores + jnp.where(
        same_page[:, :, None, :], same_bias[None, None, :, None], other_bias[None, None, :, None]
    )
    keep = valid[:, None, None, :]
    page_max = jnp.max(jnp.where(keep, scores, masked_score), axis=-1)
    weights = jnp.where(keep, jnp.exp(scores - page_max[..., None]), 0.0).astype(jnp.bfloat16)
    page_total = jnp.sum(weights, axis=-1, dtype=jnp.float32)
    page_out = jnp.einsum(
        "pthk,pkhd->pthd", weights, cache_values, preferred_element_type=jnp.float32
    )
    member = (owner[None, :] == jnp.arange(requests, dtype=jnp.int32)[:, None]) & (
        in_use[None, :] > 0
    )
    request_max = jnp.max(jnp.where(member[:, :, None, None], page_max[None], masked_score), axis=1)
    owner_max = jnp.take(request_max, owner, axis=0)
    factor = jnp.where(in_use[:, None, None] > 0, jnp.exp(page_max - owner_max), 0.0)
    member_float = member.astype(jnp.float32)
    request_total = jnp.dot(
        member_float, (page_total * factor).reshape(pool, -1), precision=highest
    ).reshape(requests, tree, head_local)
    request_out = jnp.dot(
        member_float, (page_out * factor[..., None]).reshape(pool, -1), precision=highest
    ).reshape(requests, tree, head_local, HD)
    received = (
        lax.all_to_all(request_max, "req", split_axis=0, concat_axis=0, tiled=True),
        lax.all_to_all(request_total, "req", split_axis=0, concat_axis=0, tiled=True),
        lax.all_to_all(request_out, "req", split_axis=0, concat_axis=0, tiled=True),
    )
    sources = lax.axis_size("req")
    source_max, source_total, source_out = [
        member_part.reshape((sources, local_req) + member_part.shape[1:])
        for member_part in received
    ]
    largest = jnp.max(source_max, axis=0)
    source_factor = jnp.exp(source_max - largest[None])
    cached_part = (
        largest,
        jnp.sum(source_total * source_factor, axis=0),
        jnp.sum(source_out * source_factor[..., None], axis=0),
    )
    tree_query = query.reshape(local_req, tree, head_local, HD)
    tree_key = key_new.reshape(local_req, tree, head_local, HD)
    tree_value = value_new.reshape(local_req, tree, head_local, HD)
    nodes = jnp.arange(tree, dtype=jnp.int32)
    reach = (parents[:, :, None] == nodes[None, None, :]).astype(jnp.float32) + jnp.eye(
        tree, dtype=jnp.float32
    )[None]
    for step in range(LEVELS.bit_length()):
        reach = jnp.minimum(jnp.einsum("rij,rjk->rik", reach, reach, precision=highest), 1.0)
    allowed = reach > 0.5
    group_variates = lax.dynamic_slice_in_dim(
        token_variates, req_slot * local_req * tree, local_req * tree, 0
    ).reshape(local_req, tree)
    tree_scores = (
        jnp.einsum("rihd,rjhd->rihj", tree_query, tree_key, preferred_element_type=jnp.float32)
        * scale
    )
    same_tree = group_variates[:, :, None] == group_variates[:, None, :]
    tree_scores = tree_scores + jnp.where(
        same_tree[:, :, None, :], same_bias[None, None, :, None], other_bias[None, None, :, None]
    )
    keep_tree = allowed[:, :, None, :]
    tree_max = jnp.max(jnp.where(keep_tree, tree_scores, masked_score), axis=-1)
    tree_weights = jnp.where(keep_tree, jnp.exp(tree_scores - tree_max[..., None]), 0.0).astype(
        jnp.bfloat16
    )
    tree_total = jnp.sum(tree_weights, axis=-1, dtype=jnp.float32)
    tree_out = jnp.einsum(
        "rihj,rjhd->rihd", tree_weights, tree_value, preferred_element_type=jnp.float32
    )
    final_max, final_total, final_out = merge_parts(cached_part, (tree_max, tree_total, tree_out))
    attended = (
        (final_out / final_total[..., None]).astype(jnp.bfloat16).reshape(local_req * tree, qdl)
    )
    token_heads = lax.all_to_all(attended, "head", split_axis=0, concat_axis=1, tiled=True)
    attention_rows = jnp.dot(token_heads, out_weight, preferred_element_type=jnp.float32)
    hidden_state = (tokens.astype(jnp.float32) + attention_rows).astype(jnp.bfloat16)
    normed_two = rms_scaled(hidden_state, gains[1]).astype(jnp.bfloat16)
    both_parts = jnp.einsum(
        "td,cdf->ctf",
        lax.all_gather(normed_two, "head", axis=0, tiled=True),
        gate_up_weight,
        preferred_element_type=jnp.float32,
    )
    activated = (jax.nn.silu(both_parts[0]) * both_parts[1]).astype(jnp.bfloat16)
    ffn_rows = lax.psum_scatter(
        jnp.dot(activated, down_weight, preferred_element_type=jnp.float32).astype(jnp.bfloat16),
        "head",
        scatter_dimension=0,
        tiled=True,
    ).astype(jnp.float32)
    mixed = (hidden_state.astype(jnp.float32) + ffn_rows).astype(jnp.bfloat16)
    chosen = (accepted[:, :, None] == nodes[None, None, :]).astype(jnp.bfloat16)
    stacked = jnp.stack([key_new, value_new]).reshape(2, local_req, tree, qdl)
    new_kv = jnp.einsum(
        "rat,crtq->craq", chosen, stacked, preferred_element_type=jnp.float32
    ).astype(jnp.bfloat16)
    return (mixed, attended, new_kv)


def solution(mesh):
    return jax.shard_map(
        shards,
        mesh=mesh,
        in_specs=(
            P(("req", "head"), None),
            P(),
            P(None, None, "head"),
            P(),
            P(None, None, "head"),
            P("head", None),
            P(),
            P(None, "req", None, "head"),
            P("req", None),
            P(),
            P(),
            P(),
            P("req", None),
            P("req", None),
        ),
        out_specs=(P(("req", "head"), None), P("req", "head"), P(None, "req", None, "head")),
        check_vma=False,
    )
```

profile of v0, /device:TPU:0, one launch (start us, length us, event | category | flops | bytes accessed | tf_op | source)
XLA Modules:
  0.0 184.9 jit_solution(16382638445395679382)
XLA Ops:
  7.2 2.4 %fusion.28 = (s32[20]{0:T(128)S(1)}, s32[20]{0:T(128)S(1)}, s32[20]{0:T(128)S(1)}, s32[20]{0:T(128)S(1)}) fusion(s32[8,32]{1,0:T(8,128)} %param.25, s32[20]{0:T(128)S(1)} %iota_add_fusion, s32[8]{0:T(128)} %param.24), kind=kLoop, calls=%fused_computation.64 | loop fusion | flops 46000 | bytes 1456 | tf_op jit(solution)/shard_map/reduce_sum | solution.py:76
  13.6 6.5 %all_gather.9 = bf16[64,1024]{1,0:T(8,128)(2,1)S(1)} all-gather(bf16[16,1024]{1,0:T(8,128)(2,1)S(1)} %fusion.31), channel_id=1, replica_groups=mesh['req'=8,'head'=4] {'head'}, dimensions={0}, use_global_device_ids=true | all-gather | bytes 163840 | tf_op jit(solution)/shard_map/all_gather | solution.py:65
  22.6 31.6 %all-gather = bf16[1,512,256]{2,1,0:T(8,128)(2,1)S(1)} all-gather(bf16[1,64,256]{2,1,0:T(8,128)(2,1)S(1)} %get-tuple-element.30), channel_id=2, replica_groups=mesh['req'=8,'head'=4] {'req'}, dimensions={1}, use_global_device_ids=true | all-gather | bytes 294912 | tf_op jit(solution)/shard_map/all_gather | solution.py:72
  55.1 1.9 %gather_fusion = bf16[20,64,4,64]{3,1,2,0:T(8,128)(2,1)} fusion(bf16[8,64,4,64]{3,1,2,0:T(8,128)(2,1)S(1)} %copy.74, s32[1024]{0:T(1024)S(1)} %pad_clamp_fusion), kind=kCustom, calls=%fused_computation | custom fusion | bytes 1310800 | tf_op jit(solution)/shard_map/jit(_take)/gather | solution.py:83
  57.1 3.0 %fusion.52 = (bf16[1,20,128,256]{3,2,1,0:T(8,128)(2,1)}, bf16[1,20,128,256]{3,2,1,0:T(8,128)(2,1)S(1)}) fusion(bf16[2,20,128,256]{3,2,1,0:T(8,128)(2,1)} %param.21), kind=kLoop, calls=%fused_computation.109 | loop fusion | bytes 5242880 | tf_op jit(solution)/shard_map/slice | solution.py:86
  61.9 4.2 %select_reduce_fusion = (f32[20,64,4]{1,2,0:T(4,128)S(1)}, f32[20,4,64,128]{3,2,1,0:T(8,128)}) fusion(f32[4]{0:T(128)S(1)} %get-tuple-element.34, f32[4]{0:T(128)S(1)} %get-tuple-element.33, pred[20,64,128]{2,1,0:T(8,128)(4,1)S(1)} %broadcast_compare_fusion, pred[20,128]{1,0:T(8,128)(4,1)S(1)} %iota_compare_fusion, bf16[20,128,4,64]{1,3,2,0:T(8,128)(2,1)} %bitcast.133, ...), kind=kOutput, calls=%fused_computation.9 | convolution fusion | flops 87485440 | bytes 4774452 | tf_op jit(solution)/shard_map/pthd,pkhd->pthk/dot_general | solution.py:88
  66.8 3.3 %convert_reduce_fusion = (f32[20,64,4]{1,2,0:T(4,128)S(1)}, bf16[20,64,4,128]{3,1,2,0:T(8,128)(2,1)S(1)}) fusion(f32[20,64,4]{1,2,0:T(4,128)S(1)} %get-tuple-element.35, f32[4]{0:T(128)S(1)} %get-tuple-element.34, f32[4]{0:T(128)S(1)} %get-tuple-element.33, pred[20,64,128]{2,1,0:T(8,128)(4,1)} %copy-done.1, f32[20,4,64,128]{3,2,1,0:T(8,128)} %get-tuple-element.36, ...), kind=kLoop, calls=%fused_computation.7 | loop fusion | flops 5237760 | bytes 4139552 | tf_op jit(solution)/shard_map/reduce_sum | solution.py:98
  76.6 5.4 %all-to-all-start.2 = ((f32[8,1,256]{2,1,0:T(1,128)}), f32[8,1,256]{2,1,0:T(1,128)}, u32[]{:S(2)}, u32[]{:S(2)}) async-start(f32[8,1,256]{2,1,0:T(1,128)} %reshape.533), calls=%async_computation.2 | async-start | bytes 16384 | tf_op jit(solution)/shard_map/all_to_all | solution.py:117
  84.5 2.4 %copy.76 = bf16[1,20,128,256]{2,3,1,0:T(8,128)(2,1)} copy(bf16[1,20,128,256]{3,2,1,0:T(8,128)(2,1)} %get-tuple-element.26) | data formatting | bytes 2621440 | tf_op jit(solution)/shard_map/slice | solution.py:86
  86.9 2.1 %bitcast_multiply_fusion = f32[20,64,4,64]{3,1,2,0:T(8,128)S(1)} fusion(bf16[20,64,4,128]{3,1,2,0:T(8,128)(2,1)S(1)} %get-tuple-element.25, bf16[20,128,4,64]{1,3,2,0:T(8,128)(2,1)} %bitcast.132, f32[20,64,4]{1,2,0:T(4,128)S(1)} %copy-done.4), kind=kOutput, calls=%fused_computation.5 | convolution fusion | flops 84213760 | bytes 3952640 | tf_op jit(solution)/shard_map/pthk,pkhd->pthd/dot_general | solution.py:99
  89.0 3.5 %copy.79 = f32[20,64,4,64]{3,2,1,0:T(4,128)} copy(f32[20,64,4,64]{3,1,2,0:T(8,128)S(1)} %bitcast_multiply_fusion) | data formatting | bytes 2621440 | tf_op jit(solution)/shard_map/mul | solution.py:113
  92.5 4.5 %reshape.492 = f32[20,16384]{1,0:T(8,128)} reshape(f32[20,64,4,64]{3,2,1,0:T(4,128)} %copy.79) | data formatting | bytes 2621440 | tf_op jit(solution)/shard_map/reshape | solution.py:113
  96.9 4.2 %dot_general.59 = f32[64,4,64,20]{2,1,0,3:T(4,128)} reshape(f32[16384,20]{0,1:T(8,128)} %bitcast.131) | data formatting | bytes 2621440 | tf_op jit(solution)/shard_map/dot_general | solution.py:112
  101.1 4.2 %fusion = f32[8,64,4,64]{3,0,2,1:T(8,128)S(1)} fusion(f32[64,4,64,20]{2,1,0,3:T(4,128)} %dot_general.59, s32[20]{0:T(128)S(1)} %copy-done.12, pred[20]{0:T(512)(128)(4,1)S(1)} %copy-done.9), kind=kOutput, calls=%fused_computation.3 | convolution fusion | flops 31457600 | bytes 1835108 | tf_op jit(solution)/shard_map/dot_general | solution.py:112
  106.2 6.0 %all-to-all-start.1 = ((f32[8,1,256]{2,1,0:T(1,128)}), f32[8,1,256]{2,1,0:T(1,128)S(1)}, u32[]{:S(2)}, u32[]{:S(2)}) async-start(f32[8,1,256]{2,1,0:T(1,128)} %reshape.531), calls=%async_computation.1 | async-start | bytes 16384 | tf_op jit(solution)/shard_map/all_to_all | solution.py:116
  114.4 3.0 %reshape.529 = f32[8,1,16384]{2,1,0:T(1,128)} reshape(f32[8,64,4,64]{3,2,1,0:T(4,128)} %copy.81) | data formatting | bytes 1048576
  118.7 4.7 %all-to-all-start = ((f32[8,1,16384]{2,1,0:T(1,128)}), f32[8,1,16384]{2,1,0:T(1,128)S(1)}, u32[]{:S(2)}, u32[]{:S(2)}) async-start(f32[8,1,16384]{2,1,0:T(1,128)} %reshape.529), calls=%async_computation | async-start | bytes 1048576 | tf_op jit(solution)/shard_map/all_to_all | solution.py:118
  129.2 4.5 %all-to-all-done = f32[8,1,16384]{2,1,0:T(1,128)S(1)} async-done(((f32[8,1,16384]{2,1,0:T(1,128)}), f32[8,1,16384]{2,1,0:T(1,128)S(1)}, u32[]{:S(2)}, u32[]{:S(2)}) %all-to-all-start) | async-done | bytes 524320 | tf_op jit(solution)/shard_map/all_to_all | solution.py:118
  133.7 2.8 %reduce.8 = f32[8,16384]{1,0:T(8,128)} reduce(f32[8,1,16384]{2,1,0:T(1,128)S(1)} %all-to-all-done, f32[]{:T(128)} %broadcast.354), dimensions={1}, to_apply=%all_to_all.23.reduce_sub_computation | reduce | bytes 1048580 | tf_op jit(solution)/shard_map/all_to_all | solution.py:118
  140.4 6.5 %all_to_all.34 = bf16[4,16,256]{2,1,0:T(8,128)(2,1)S(1)} all-to-all(bf16[4,16,256]{2,1,0:T(8,128)(2,1)S(1)} %all_to_all.26), channel_id=1, replica_groups=mesh['req'=8,'head'=4] {'head'}, dimensions={0} | all-to-all | bytes 65536 | tf_op jit(solution)/shard_map/all_to_all | solution.py:166
  146.9 2.1 %multiply_reduce_fusion.1 = (f32[16]{0:T(128)S(1)}, f32[16,1024]{1,0:T(8,128)S(1)}) fusion(bf16[16,1024]{1,0:T(8,128)(2,1)S(1)} %bitcast.140, bf16[1024,1024]{1,0:T(8,128)(2,1)} %param.17, bf16[16,1024]{1,0:T(8,128)(2,1)} %param.14), kind=kOutput, calls=%fused_computation.73 | convolution fusion | flops 33652720 | bytes 2228288 | tf_op jit(solution)/shard_map/dot_general | solution.py:167
  149.1 5.4 %all_gather.11 = bf16[64,1024]{1,0:T(8,128)(2,1)S(1)} all-gather(bf16[16,1024]{1,0:T(8,128)(2,1)S(1)} %multiply_convert_fusion), channel_id=1, replica_groups=mesh['req'=8,'head'=4] {'head'}, dimensions={0}, use_global_device_ids=true | all-gather | bytes 163840 | tf_op jit(solution)/shard_map/all_gather | solution.py:172
  154.5 3.0 %convolution_bitcast_fusion = f32[2,64,1024]{2,1,0:T(8,128)S(1)} fusion(bf16[2,1024,1024]{2,1,0:T(8,128)(2,1)} %param.18, bf16[64,1024]{1,0:T(8,128)(2,1)S(1)} %all_gather.11), kind=kOutput, calls=%fused_computation.13 | convolution fusion | flops 268435456 | bytes 4849664 | tf_op jit(solution)/shard_map/td,cdf->ctf/dot_general | solution.py:170
  160.2 16.4 %reduce-scatter.2.cloned.1.call-done = bf16[16,1024]{1,0:T(8,128)(2,1)} async-done(((bf16[64,1024]{1,0:T(8,128)(2,1)}), bf16[16,1024]{1,0:T(8,128)(2,1)}) %reduce-scatter.2.cloned.1.call-update) | async-done | bytes 32784 | tf_op jit(solution)/shard_map/reduce_scatter | solution.py:177
  (120 shorter events, 36.9 us)
Async XLA Ops:
  7.2 150.4 %copy-start = (bf16[1024,1024]{1,0:T(8,128)(2,1)S(1)}, bf16[1024,1024]{1,0:T(8,128)(2,1)}, u32[]{:S(2)}) copy-start(bf16[1024,1024]{1,0:T(8,128)(2,1)} %param.19) | copy-start | bytes 6291460
  9.6 61.3 %copy-start.11 = (s32[20]{0:T(128)}, s32[20]{0:T(128)S(1)}, u32[]{:S(2)}) copy-start(s32[20]{0:T(128)S(1)} %get-tuple-element.18) | copy-start | bytes 244
  9.6 52.2 %copy-start.14 = (pred[20]{0:T(512)(128)(4,1)}, pred[20]{0:T(512)(128)(4,1)S(1)}, u32[]{:S(2)}) copy-start(pred[20]{0:T(512)(128)(4,1)S(1)} %get-tuple-element.41) | copy-start | bytes 64
  9.7 61.3 %copy-start.8 = (pred[20]{0:T(512)(128)(4,1)}, pred[20]{0:T(512)(128)(4,1)S(1)}, u32[]{:S(2)}) copy-start(pred[20]{0:T(512)(128)(4,1)S(1)} %get-tuple-element.42) | copy-start | bytes 64
  9.7 47.3 %copy-start.15 = (s32[1024]{0:T(1024)}, s32[1024]{0:T(1024)S(1)}, u32[]{:S(2)}) copy-start(s32[1024]{0:T(1024)S(1)} %pad_clamp_fusion) | copy-start | bytes 12292
  21.9 35.1 %copy-start.20 = (f32[2,16]{1,0:T(2,128)S(1)}, f32[2,16]{1,0:T(2,128)}, u32[]{:S(2)}) copy-start(f32[2,16]{1,0:T(2,128)} %param.20) | copy-start | bytes 388
  57.1 9.8 %copy-start.16 = (f32[4]{0:T(128)}, f32[4]{0:T(128)S(1)}, u32[]{:S(2)}) copy-start(f32[4]{0:T(128)S(1)} %get-tuple-element.33) | copy-start | bytes 52
  57.1 9.8 %copy-start.18 = (f32[4]{0:T(128)}, f32[4]{0:T(128)S(1)}, u32[]{:S(2)}) copy-start(f32[4]{0:T(128)S(1)} %get-tuple-element.34) | copy-start | bytes 52
  60.1 1.5 copy-start.13
  61.9 4.2 %copy-start.1 = (pred[20,64,128]{2,1,0:T(8,128)(4,1)}, pred[20,64,128]{2,1,0:T(8,128)(4,1)S(1)}, u32[]{:S(2)}) copy-start(pred[20,64,128]{2,1,0:T(8,128)(4,1)S(1)} %broadcast_compare_fusion) | copy-start | bytes 491524
  76.6 29.6 %all-to-all-start.2 = ((f32[8,1,256]{2,1,0:T(1,128)}), f32[8,1,256]{2,1,0:T(1,128)}, u32[]{:S(2)}, u32[]{:S(2)}) async-start(f32[8,1,256]{2,1,0:T(1,128)} %reshape.533), calls=%async_computation.2 | async-start | bytes 16384 | tf_op jit(solution)/shard_map/all_to_all | solution.py:117
  84.5 2.5 %copy-start.4 = (f32[20,64,4]{1,2,0:T(4,128)S(1)}, f32[20,64,4]{1,2,0:T(4,128)}, u32[]{:S(2)}) copy-start(f32[20,64,4]{1,2,0:T(4,128)} %exponential_select_fusion) | copy-start | bytes 61444
  96.9 4.2 %copy-start.9 = (pred[20]{0:T(512)(128)(4,1)S(1)}, pred[20]{0:T(512)(128)(4,1)}, u32[]{:S(2)}) copy-start(pred[20]{0:T(512)(128)(4,1)} %copy-done.8) | copy-start | bytes 64
  96.9 4.2 %copy-start.12 = (s32[20]{0:T(128)S(1)}, s32[20]{0:T(128)}, u32[]{:S(2)}) copy-start(s32[20]{0:T(128)} %copy-done.11) | copy-start | bytes 244
  105.3 18.6 %copy-start.7 = (bf16[1,64,256]{2,1,0:T(8,128)(2,1)S(1)}, bf16[1,64,256]{2,1,0:T(8,128)(2,1)}, u32[]{:S(2)}) copy-start(bf16[1,64,256]{2,1,0:T(8,128)(2,1)} %get-tuple-element.28) | copy-start | bytes 98308
  105.3 18.8 %copy-start.6 = (bf16[1,64,256]{2,1,0:T(8,128)(2,1)S(1)}, bf16[1,64,256]{2,1,0:T(8,128)(2,1)}, u32[]{:S(2)}) copy-start(bf16[1,64,256]{2,1,0:T(8,128)(2,1)} %get-tuple-element.29) | copy-start | bytes 98308
  105.5 19.3 %copy-start.17 = (f32[4]{0:T(128)S(1)}, f32[4]{0:T(128)}, u32[]{:S(2)}) copy-start(f32[4]{0:T(128)} %copy-done.16) | copy-start | bytes 52
  105.5 19.3 %copy-start.19 = (f32[4]{0:T(128)S(1)}, f32[4]{0:T(128)}, u32[]{:S(2)}) copy-start(f32[4]{0:T(128)} %copy-done.18) | copy-start | bytes 52
  106.2 12.5 %all-to-all-start.1 = ((f32[8,1,256]{2,1,0:T(1,128)}), f32[8,1,256]{2,1,0:T(1,128)S(1)}, u32[]{:S(2)}, u32[]{:S(2)}) async-start(f32[8,1,256]{2,1,0:T(1,128)} %reshape.531), calls=%async_computation.1 | async-start | bytes 16384 | tf_op jit(solution)/shard_map/all_to_all | solution.py:116
  118.7 15.0 %all-to-all-start = ((f32[8,1,16384]{2,1,0:T(1,128)}), f32[8,1,16384]{2,1,0:T(1,128)S(1)}, u32[]{:S(2)}, u32[]{:S(2)}) async-start(f32[8,1,16384]{2,1,0:T(1,128)} %reshape.529), calls=%async_computation | async-start | bytes 1048576 | tf_op jit(solution)/shard_map/all_to_all | solution.py:118
  123.4 53.2 %reduce-scatter.2.cloned.1.call-start = ((), (), s32[]{:S(2)}) async-start(), calls=%async_computation.5 | async-start | bytes 163840 | tf_op jit(solution)/shard_map/reduce_scatter | solution.py:177
  138.2 10.8 %copy-start.10 = (f32[1,1024]{1,0:T(1,128)S(1)}, f32[1,1024]{1,0:T(1,128)}, u32[]{:S(2)}) copy-start(f32[1,1024]{1,0:T(1,128)} %get-tuple-element.31) | copy-start | bytes 12292
  157.6 1.2 copy-start.3
  157.6 1.2 copy-start.21
  (2 other events, 1.3 us)
Sparse Core Ops, SparseCore 0:
  158.8 17.7 reduce-scatter.1
where the time goes:
time: 186 us; the launch traced here: 185 us
  blocking collectives  50 us (27%)
  local copies, waits for them, and re-layouts  40.9 us (22%)
  waiting for transfers between devices  22.2 us (12%)
  matrix products  22 us (12%)
  other arithmetic  19 us (10%)
  starting transfers between devices  16.3 us (9%)
  between operations  14.5 us (8%)
    all_gather x1, blocking collectives, shards(): all_queries = lax.all_gather(query, 'req', axis=0, tiled=True)  31.6 us
    reduce_scatter x1, waiting for transfers between devices, shards(): lax.psum_scatter(jnp.dot(activated, down_weight, preferred_element_type=j...  16.4 us
    unnamed x51, local copies, waits for them, and re-layouts  8.42 us
    all_to_all x1, blocking collectives, shards(): lax.all_to_all(attended, 'head', split_axis=0, concat_axis=1, tiled=True)  6.5 us
    all_gather x1, blocking collectives, shards(): lax.all_gather(normed, 'head', axis=0, tiled=True)  6.47 us
    all_to_all x1, starting transfers between devices, shards(): lax.all_to_all(request_max, 'req', split_axis=0, concat_axis=0, tiled=True)  6 us
    slice x2, local copies, waits for them, and re-layouts, shards(): cache_values = page_cache[1].reshape(pool, page, head_local, HD)  5.47 us
    dot_general x2, local copies, waits for them, and re-layouts, shards(): jnp.dot(member_float, (page_out * factor[..., None]).reshape(pool, -1), p...  5.46 us
  transfers between devices with their start and end apart: 4, of which 3 were waited for; matrix products, arithmetic and copies ran while one was open for 19% of the time, Pallas kernels for 0%

commit v1 on v0

v1 whole, which is shorter than its diff:
```python
import functools
import math

import jax
import jax.numpy as jnp
from jax import lax
from jax.experimental import pallas as pl
from jax.experimental.pallas import tpu as pltpu
from jax.sharding import PartitionSpec as P

HD = 64
NVAR = 4
TERMS = 3
BROWS = 16
epsilon = 1e-06
low = -1e30
f32 = jnp.float32
bf16 = jnp.bfloat16


def rms_scaled(values, gain):
    return values * lax.rsqrt(jnp.mean(values * values, axis=-1, keepdims=True) + epsilon) * gain


def iota(shape, dim):
    return lax.broadcasted_iota(jnp.int32, shape, dim)


def dot(a, b, ca=1, cb=0):
    return lax.dot_general(a, b, (((ca,), (cb,)), ((), ())), preferred_element_type=f32)


def kernel(
    R, H,
    tokens, gains, qkv_hbm, out_hbm, gu_hbm, down_hbm, vbias, cache_hbm, pvar, tvar, clen, ptab, parents, accepted,
    mixed, attended, new_kv,
    qkv, outw, gu, downw, pages, tbuf, qbuf, tvoh, bmat, oh, own_s, fill_s, own_rows, pm, plt, po,
    osend, ssend, obuf, sbuf, gbuf, act, hid, dsend, dbuf,
    lsem, ts, tr, qs, qr, os_, or_, ss, sr, gs, gr, ds_, dr,
):
    req = lax.axis_index("req")
    head = lax.axis_index("head")
    rows, D = tokens.shape
    QL = qkv.shape[2]
    HL = QL // HD
    pool, page = pvar.shape
    maxp = ptab.shape[1]
    tree = parents.shape[1]
    C = HL * tree
    FFL = gu.shape[2]

    def at_head(d):
        return {"req": req, "head": lax.rem(head + d, H)}

    def at_req(d):
        return {"req": lax.rem(req + d, R), "head": head}

    def remote(src, dst, s, r, device):
        return pltpu.make_async_remote_copy(
            src_ref=src, dst_ref=dst, send_sem=s, recv_sem=r, device_id=device, device_id_type=pl.DeviceIdType.MESH
        )

    barrier = pltpu.get_barrier_semaphore()
    for d in range(1, H):
        pl.semaphore_signal(barrier, inc=1, device_id=at_head(d), device_id_type=pl.DeviceIdType.MESH)

    @pl.loop(1, R)
    def _(d):
        pl.semaphore_signal(barrier, inc=1, device_id=at_req(d), device_id_type=pl.DeviceIdType.MESH)

    own_tokens = pltpu.make_async_copy(tokens, tbuf.at[head], lsem.at[0])
    own_tokens.start()
    get_qkv = pltpu.make_async_copy(qkv_hbm, qkv, lsem.at[1])
    get_qkv.start()
    get_pages = pltpu.make_async_copy(cache_hbm, pages, lsem.at[2])
    get_pages.start()
    get_out = pltpu.make_async_copy(out_hbm, outw, lsem.at[3])
    get_gu = pltpu.make_async_copy(gu_hbm, gu, lsem.at[4])
    get_down = pltpu.make_async_copy(down_hbm, downw, lsem.at[5])
    get_out.start()
    get_gu.start()
    get_down.start()
    pl.semaphore_wait(barrier, H - 1 + R - 1)

    token_copies = [
        remote(tokens, tbuf.at[head], ts.at[d - 1], tr.at[d - 1], at_head(d)) for d in range(1, H)
    ]
    for copy in token_copies:
        copy.start()

    table = ptab[...]
    place = iota(table.shape, 0) * maxp + iota(table.shape, 1) + 1
    row16 = iota((BROWS, page), 0)
    lane16 = iota((BROWS, page), 1)
    own_rows[...] = jnp.full(own_rows.shape, -1, jnp.int32)
    pm[...] = jnp.zeros(pm.shape, f32)
    plt[...] = jnp.zeros(plt.shape, f32)

    @pl.loop(0, pool)
    def _(p):
        code = jnp.max(jnp.where(table == req * pool + p, place, 0))
        used = code > 0
        slot = jnp.maximum(code - 1, 0)
        owner = slot // maxp
        filled = jnp.where(used, jnp.clip(clen[owner] - (slot - owner * maxp) * page, 0, page), 0)
        own_s[p] = owner
        fill_s[p] = filled
        own_rows[pl.ds(p, 1), :] = jnp.full((1, C), jnp.where(used, owner, -1), jnp.int32)
        line = pvar[pl.ds(p, 1), :]
        hot = jnp.where(row16 < TERMS * NVAR, (line == row16 % NVAR).astype(f32), 0.0)
        hot = jnp.where(row16 == TERMS * NVAR, (lane16 >= filled).astype(f32), hot)
        oh[p] = hot.astype(bf16)

    lane_head = iota((1, C), 1) // tree
    same_row = jnp.zeros((1, C), f32)
    other_row = jnp.zeros((1, C), f32)
    for h in range(HL):
        same_row = jnp.where(lane_head == h, vbias[0, head * HL + h], same_row)
        other_row = jnp.where(lane_head == h, vbias[1, head * HL + h], other_row)

    def split(row):
        one = row.astype(bf16).astype(f32)
        two = (row - one).astype(bf16).astype(f32)
        three = (row - one - two).astype(bf16).astype(f32)
        term = iota((BROWS, C), 0) // NVAR
        return jnp.where(term == 0, one, jnp.where(term == 1, two, jnp.where(term == 2, three, 0.0)))

    same_terms = split(same_row)
    other_terms = split(other_row)
    spread = (iota((tree, C), 0) == iota((tree, C), 1) % tree).astype(f32).astype(bf16)
    brow = iota((BROWS, C), 0)
    trow = iota((BROWS, tree), 0)
    for r in range(R):
        line = tvar[:, r * tree : (r + 1) * tree]
        hot = jnp.where(trow < TERMS * NVAR, (line == trow % NVAR).astype(f32), 0.0).astype(bf16)
        tvoh[r] = hot
        matched = dot(hot, spread) > 0.5
        terms = jnp.where(matched, same_terms, other_terms)
        bmat[r] = jnp.where(brow == TERMS * NVAR, low, terms).astype(bf16)

    up = parents[...]
    eye = (iota((tree, tree), 0) == iota((tree, tree), 1)).astype(f32)
    reach = ((iota((tree, tree), 0) == up).astype(f32) + eye).astype(bf16)
    clip = lambda v: jnp.minimum(v, 1.0).astype(bf16)
    reach2 = clip(dot(reach, reach))
    reach4 = clip(dot(reach2, reach2))
    reach8 = clip(dot(reach4, reach4))
    allowed = dot(reach8, spread) > 0.5

    block = (iota((C, QL), 0) // tree == iota((C, QL), 1) // HD).astype(f32).astype(bf16)

    own_tokens.wait()
    for copy in token_copies:
        copy.wait()
    get_qkv.wait()
    values = tbuf[...].astype(f32).reshape(H * rows, D)
    normed = rms_scaled(values, gains[0:1, :]).astype(bf16)
    scale = 1.0 / math.sqrt(HD)
    query = (dot(normed, qkv[0]).astype(bf16).astype(f32) * scale).astype(bf16)
    qbuf[req] = query

    def query_copy(d):
        return remote(qbuf.at[req], qbuf.at[req], qs.at[d], qr.at[d], at_req(d))

    @pl.loop(1, R)
    def _(d):
        query_copy(d).start()

    keys = dot(normed, qkv[1]).astype(bf16)
    vals = dot(normed, qkv[2]).astype(bf16)
    chosen = (iota((tree, accepted.shape[1]), 0) == accepted[...]).astype(f32).astype(bf16)
    new_kv[0, 0] = dot(chosen, keys, 0, 0).astype(bf16)
    new_kv[1, 0] = dot(chosen, vals, 0, 0).astype(bf16)

    def spread_query(q):
        return jnp.concatenate([q] * HL, axis=0) * block

    head_lanes = iota((HD, C), 1) // tree

    def pick(wide):
        out = wide[0:HD]
        for h in range(1, HL):
            out = jnp.where(head_lanes == h, wide[h * HD : (h + 1) * HD], out)
        return out

    tree_scores = dot(keys, spread_query(query), 1, 1) + dot(tvoh[req], bmat[req], 0, 0)
    tree_max = jnp.max(jnp.where(allowed, tree_scores, low), axis=0, keepdims=True)
    tree_w = jnp.where(allowed, jnp.exp(tree_scores - tree_max), 0.0).astype(bf16)
    tree_total = jnp.sum(tree_w.astype(f32), axis=0, keepdims=True)
    tree_out = pick(dot(vals, tree_w, 0, 0))

    get_pages.wait()

    @pl.loop(1, R)
    def _(d):
        query_copy(d).wait()

    group = 4 if pool % 4 == 0 else 1

    @pl.loop(0, pool // group)
    def _(g):
        for k in range(group):
            p = g * group + k
            owner = own_s[p]
            scores = dot(pages[0, p], spread_query(qbuf[owner]), 1, 1) + dot(oh[p], bmat[owner], 0, 0)
            top = jnp.max(scores, axis=0, keepdims=True)
            w = jnp.exp(scores - top).astype(bf16)
            pm[pl.ds(p, 1), :] = top
            plt[pl.ds(p, 1), :] = jnp.sum(w.astype(f32), axis=0, keepdims=True)
            po[p] = pick(dot(pages[1, p], w, 0, 0))

    def out_copy(d):
        return remote(osend.at[d], obuf.at[d], os_.at[d], or_.at[d], at_req(d))

    def stat_copy(d):
        return remote(ssend.at[d], sbuf.at[d], ss.at[d], sr.at[d], at_req(d))

    def merged(r):
        mask = own_rows[...] == r
        maxes = pm[...]
        top = jnp.max(jnp.where(mask, maxes, low), axis=0, keepdims=True)
        factor = jnp.where(mask, jnp.exp(maxes - top), 0.0)
        total = jnp.sum(factor * plt[...], axis=0, keepdims=True)
        out = factor[0:1] * po[0]
        for p in range(1, pool):
            out = out + factor[p : p + 1] * po[p]
        return top, total, out

    srow = iota((8, C), 0)

    @pl.loop(1, R)
    def _(d):
        top, total, out = merged(lax.rem(req + d, R))
        osend[d] = out.astype(bf16)
        ssend[d] = jnp.where(srow == 0, top, total)
        out_copy(d).start()
        stat_copy(d).start()

    top, total, out = merged(req)
    new_top = jnp.maximum(top, tree_max)
    fa = jnp.exp(top - new_top)
    fb = jnp.exp(tree_max - new_top)
    osend[0] = jnp.zeros((HD, C), bf16)
    total = total * fa + tree_total * fb
    out = out * fa + tree_out * fb
    top = new_top

    @pl.loop(1, R)
    def _(d):
        out_copy(d).wait()
        stat_copy(d).wait()

    final_top = top
    for d in range(1, R):
        final_top = jnp.maximum(final_top, sbuf[d][0:1])
    fa = jnp.exp(top - final_top)
    total = total * fa
    out = out * fa
    for d in range(1, R):
        stats = sbuf[d]
        fd = jnp.exp(stats[0:1] - final_top)
        total = total + stats[1:2] * fd
        out = out + obuf[d].astype(f32) * fd
    att_t = (out / total).astype(bf16)
    diag = jnp.concatenate([att_t] * HL, axis=0) * (
        iota((HL * HD, C), 0) // HD == iota((HL * HD, C), 1) // tree
    ).astype(f32).astype(bf16)
    att = dot(spread, diag, 1, 1).astype(bf16)
    gbuf[head] = att
    att_copies = [remote(gbuf.at[head], gbuf.at[head], gs.at[d - 1], gr.at[d - 1], at_head(d)) for d in range(1, H)]
    for copy in att_copies:
        copy.start()
    attended[...] = att
    get_out.wait()
    state = values + dot(att, outw[pl.ds(pl.multiple_of(head * QL, QL), QL), :])
    for d in range(1, H):
        att_copies[d - 1].wait()
        source = lax.rem(head + H - d, H)
        state = state + dot(gbuf[source], outw[pl.ds(pl.multiple_of(source * QL, QL), QL), :])
    state = state.astype(bf16).astype(f32)
    hid[...] = state.reshape(H, rows, D)
    normed_two = rms_scaled(state, gains[1:2, :]).astype(bf16)
    get_gu.wait()
    step = 256
    for c in range(0, FFL, step):
        gate = dot(normed_two, gu[0, :, c : c + step])
        upward = dot(normed_two, gu[1, :, c : c + step])
        act[:, c : c + step] = (gate / (1.0 + jnp.exp(-gate)) * upward).astype(bf16)
    get_down.wait()
    activated = act[...]
    for c in range(0, D, step):
        part = dot(activated, downw[:, c : c + step])
        dsend[:, :, c : c + step] = part.reshape(H, rows, step).astype(bf16)
    down_copies = [
        remote(dsend.at[lax.rem(head + d, H)], dbuf.at[d - 1], ds_.at[d - 1], dr.at[d - 1], at_head(d))
        for d in range(1, H)
    ]
    for copy in down_copies:
        copy.start()
    result = dsend[head].astype(f32)
    for d in range(1, H):
        down_copies[d - 1].wait()
        result = result + dbuf[d - 1].astype(f32)
    mixed[...] = (hid[head] + result).astype(bf16)


def shards(
    tokens, gains, qkv_weight, out_weight, gate_up_weight, down_weight, variate_bias, page_cache, page_variates,
    token_variates, cache_len, page_table, parents, accepted,
):
    R = lax.axis_size("req")
    H = lax.axis_size("head")
    rows, D = tokens.shape
    QL = qkv_weight.shape[2]
    HL = QL // HD
    pool, page = page_variates.shape
    tree = parents.shape[1]
    C = HL * tree
    padded = (pool + 7) // 8 * 8
    hbm = pl.BlockSpec(memory_space=pl.ANY)
    vmem = pl.BlockSpec(memory_space=pltpu.VMEM)
    smem = pl.BlockSpec(memory_space=pltpu.SMEM)
    dma = pltpu.SemaphoreType.DMA
    return tuple(pl.pallas_call(
        functools.partial(kernel, R, H),
        out_shape=(
            jax.ShapeDtypeStruct((rows, D), bf16),
            jax.ShapeDtypeStruct((tree, QL), bf16),
            jax.ShapeDtypeStruct((2, 1, accepted.shape[1], QL), bf16),
        ),
        in_specs=[hbm, vmem, hbm, hbm, hbm, hbm, smem, hbm, vmem, vmem, smem, vmem, vmem, vmem],
        out_specs=(vmem, vmem, vmem),
        scratch_shapes=[
            pltpu.VMEM(qkv_weight.shape, bf16),
            pltpu.VMEM(out_weight.shape, bf16),
            pltpu.VMEM(gate_up_weight.shape, bf16),
            pltpu.VMEM(down_weight.shape, bf16),
            pltpu.VMEM(page_cache.shape, bf16),
            pltpu.VMEM((H, rows, D), bf16),
            pltpu.VMEM((R, tree, QL), bf16),
            pltpu.VMEM((R, BROWS, tree), bf16),
            pltpu.VMEM((R, BROWS, C), bf16),
            pltpu.VMEM((pool, BROWS, page), bf16),
            pltpu.SMEM((pool,), jnp.int32),
            pltpu.SMEM((pool,), jnp.int32),
            pltpu.VMEM((padded, C), jnp.int32),
            pltpu.VMEM((padded, C), f32),
            pltpu.VMEM((padded, C), f32),
            pltpu.VMEM((pool, HD, C), f32),
            pltpu.VMEM((R, HD, C), bf16),
            pltpu.VMEM((R, 8, C), f32),
            pltpu.VMEM((R, HD, C), bf16),
            pltpu.VMEM((R, 8, C), f32),
            pltpu.VMEM((H, tree, QL), bf16),
            pltpu.VMEM((tree, gate_up_weight.shape[2]), bf16),
            pltpu.VMEM((H, rows, D), f32),
            pltpu.VMEM((H, rows, D), bf16),
            pltpu.VMEM((H, rows, D), bf16),
            dma((6,)),
            dma((H,)), dma((H,)),
            dma((R,)), dma((R,)),
            dma((R,)), dma((R,)),
            dma((R,)), dma((R,)),
            dma((H,)), dma((H,)),
            dma((H,)), dma((H,)),
        ],
        compiler_params=pltpu.CompilerParams(
            collective_id=0, has_side_effects=True, vmem_limit_bytes=52 * 1024 * 1024
        ),
        cost_estimate=pl.CostEstimate(flops=10**9, bytes_accessed=12 * 10**6, transcendentals=10**6),
    )(
        tokens, gains, qkv_weight, out_weight, gate_up_weight, down_weight, variate_bias, page_cache, page_variates,
        token_variates.reshape(1, -1), cache_len, page_table, parents, accepted,
    ))


def solution(mesh):
    return jax.shard_map(
        shards,
        mesh=mesh,
        in_specs=(
            P(("req", "head"), None),
            P(),
            P(None, None, "head"),
            P(),
            P(None, None, "head"),
            P("head", None),
            P(),
            P(None, "req", None, "head"),
            P("req", None),
            P(),
            P(),
            P(),
            P("req", None),
            P("req", None),
        ),
        out_specs=(P(("req", "head"), None), P("req", "head"), P(None, "req", None, "head")),
        check_vma=False,
    )
```

time: 186 us -> 51.9 us (0.28)
  blocking collectives: 50 us -> 0 us
  Pallas kernels: 0 us -> 41.4 us
  local copies, waits for them, and re-layouts: 40.9 us -> 9.4 us
  waiting for transfers between devices: 22.2 us -> 0 us
  matrix products: 22 us -> 0 us
  other arithmetic: 19 us -> 0 us
  starting transfers between devices: 16.3 us -> 0 us
  between operations: 14.5 us -> 0.66 us
    all_gather x3 -> x0, blocking collectives: 43.5 us -> none  [the longest x1 31.6 us: shards(): all_queries = lax.all_gather(query, 'req', axis=0, tiled=True)]
    pallas_call x0 -> x1, Pallas kernels: none -> 41.4 us  [shards(): pl.pallas_call(functools.partial(kernel, R, H), out_shape=(jax.ShapeDtype...]
    dot_general x15 -> x0, matrix products: 22 us -> none  [the longest x1 4.2 us: shards(): jnp.einsum('pthd,pkhd->pthk', page_queries, cache_keys, preferred_element...]
    reduce_scatter x1 -> x0, waiting for transfers between devices: 16.4 us -> none  [shards(): lax.psum_scatter(jnp.dot(activated, down_weight, preferred_element_type=j...]
    all_to_all x3 -> x0, starting transfers between devices: 16 us -> none  [the longest x1 6 us: shards(): lax.all_to_all(request_max, 'req', split_axis=0, concat_axis=0, tiled=True)]
    slice x5 -> x0, local copies, waits for them, and re-layouts: 8.92 us -> none  [the longest x2 5.47 us: shards(): cache_values = page_cache[1].reshape(pool, page, head_local, HD)]
    reduce_sum x6 -> x0, other arithmetic: 7.45 us -> none  [the longest x1 3.34 us: shards(): page_total = jnp.sum(weights, axis=-1, dtype=jnp.float32)]
    all_to_all x1 -> x0, blocking collectives: 6.5 us -> none  [shards(): lax.all_to_all(attended, 'head', split_axis=0, concat_axis=1, tiled=True)]
  transfers between devices with their start and end apart: 4 -> 0, of which waited for: 3 -> 0; matrix products, arithmetic and copies ran while one was open for 19% -> 0% of each run, Pallas kernels for 0% -> 0%
where the time goes in v1:
time: 51.9 us; the launch traced here: 51.5 us
  Pallas kernels  41.4 us (80%)
  local copies, waits for them, and re-layouts  9.4 us (18%)
  between operations  0.66 us (1%)
    pallas_call x1, Pallas kernels, shards(): pl.pallas_call(functools.partial(kernel, R, H), out_shape=(jax.ShapeDtype...  41.4 us
    unnamed x23, local copies, waits for them, and re-layouts  9.4 us

profile of v1, /device:TPU:0, one launch (start us, length us, event | category | flops | bytes accessed | tf_op | source)
XLA Modules:
  0.0 51.5 jit_solution(5830685176462375074)
XLA Ops:
  0.6 0.0 copy-start
  0.6 1.4 %copy-done = bf16[3,1024,256]{2,1,0:T(8,128)(2,1)S(1)} copy-done((bf16[3,1024,256]{2,1,0:T(8,128)(2,1)S(1)}, bf16[3,1024,256]{2,1,0:T(8,128)(2,1)}, u32[]{:S(2)}) %copy-start) | copy-done | bytes 1572888
  2.0 0.0 copy-start.1
  2.0 0.8 %copy-done.1 = bf16[16,1024]{1,0:T(8,128)(2,1)S(1)} copy-done((bf16[16,1024]{1,0:T(8,128)(2,1)S(1)}, bf16[16,1024]{1,0:T(8,128)(2,1)}, u32[]{:S(2)}) %copy-start.1) | copy-done | bytes 32792
  2.8 0.0 copy-start.2
  2.8 0.7 %copy-done.2 = s32[20,128]{1,0:T(8,128)S(1)} copy-done((s32[20,128]{1,0:T(8,128)S(1)}, s32[20,128]{1,0:T(8,128)}, u32[]{:S(2)}) %copy-start.2) | copy-done | bytes 10264
  3.5 0.0 copy-start.3
  3.5 0.7 %copy-done.3 = f32[2,1024]{1,0:T(2,128)S(1)} copy-done((f32[2,1024]{1,0:T(2,128)S(1)}, f32[2,1024]{1,0:T(2,128)}, u32[]{:S(2)}) %copy-start.3) | copy-done | bytes 8216
  4.2 0.0 copy-start.4
  4.2 0.7 %copy-done.4 = s32[8,32]{1,0:T(8,128)S(1)} copy-done((s32[8,32]{1,0:T(8,128)S(1)}, s32[8,32]{1,0:T(8,128)}, u32[]{:S(2)}) %copy-start.4) | copy-done | bytes 1048
  4.9 0.0 copy-start.5
  4.9 0.7 %copy-done.5 = s32[512]{0:T(512)S(1)} copy-done((s32[512]{0:T(512)S(1)}, s32[512]{0:T(512)}, u32[]{:S(2)}) %copy-start.5) | copy-done | bytes 2072
  5.6 0.0 copy-start.6
  5.6 0.7 %copy-done.6 = f32[2,16]{1,0:T(2,128)S(1)} copy-done((f32[2,16]{1,0:T(2,128)S(1)}, f32[2,16]{1,0:T(2,128)}, u32[]{:S(2)}) %copy-start.6) | copy-done | bytes 152
  6.3 0.0 copy-start.7
  6.3 0.7 %copy-done.7 = s32[8]{0:T(128)S(1)} copy-done((s32[8]{0:T(128)S(1)}, s32[8]{0:T(128)}, u32[]{:S(2)}) %copy-start.7) | copy-done | bytes 56
  6.9 0.0 copy-start.8
  6.9 0.7 %copy-done.8 = s32[1,64]{1,0:T(1,128)S(1)} copy-done((s32[1,64]{1,0:T(1,128)S(1)}, s32[1,64]{1,0:T(1,128)}, u32[]{:S(2)}) %copy-start.8) | copy-done | bytes 280
  7.6 0.0 copy-start.9
  7.6 0.7 %copy-done.9 = s32[1,8]{1,0:T(1,128)S(1)} copy-done((s32[1,8]{1,0:T(1,128)S(1)}, s32[1,8]{1,0:T(1,128)}, u32[]{:S(2)}) %copy-start.9) | copy-done | bytes 56
  8.2 41.4 %shard_map.157 = (bf16[16,1024]{1,0:T(8,128)(2,1)S(1)}, bf16[64,256]{1,0:T(8,128)(2,1)S(1)}, bf16[2,1,8,256]{3,2,1,0:T(8,128)(2,1)S(1)}) custom-call(bf16[16,1024]{1,0:T(8,128)(2,1)S(1)} %copy-done.1, f32[2,1024]{1,0:T(2,128)S(1)} %copy-done.3, bf16[3,1024,256]{2,1,0:T(8,128)(2,1)S(1)} %copy-done, bf16[1024,1024]{1,0:T(8,128)(2,1)} %out_hbm.1, ...), custom_call_target="tpu_custom_call" | custom-call | flops 1000000000 | bytes 12000000 | tf_op jit(solution)/shard_map/pallas_call | solution.py:324
  49.7 0.6 %copy.20 = bf16[16,1024]{1,0:T(8,128)(2,1)} copy(bf16[16,1024]{1,0:T(8,128)(2,1)S(1)} %get-tuple-element.6) | data formatting | bytes 65536
  50.3 0.6 %copy.21 = bf16[64,256]{1,0:T(8,128)(2,1)} copy(bf16[64,256]{1,0:T(8,128)(2,1)S(1)} %get-tuple-element.7) | data formatting | bytes 65536
  50.9 0.6 %copy.22 = bf16[2,1,8,256]{3,2,1,0:T(8,128)(2,1)} copy(bf16[2,1,8,256]{3,2,1,0:T(8,128)(2,1)S(1)} %get-tuple-element.8) | data formatting | bytes 16384
Async XLA Ops:
  0.6 1.4 %copy-start = (bf16[3,1024,256]{2,1,0:T(8,128)(2,1)S(1)}, bf16[3,1024,256]{2,1,0:T(8,128)(2,1)}, u32[]{:S(2)}) copy-start(bf16[3,1024,256]{2,1,0:T(8,128)(2,1)} %qkv_hbm.1) | copy-start | bytes 4718596
  2.0 0.8 %copy-start.1 = (bf16[16,1024]{1,0:T(8,128)(2,1)S(1)}, bf16[16,1024]{1,0:T(8,128)(2,1)}, u32[]{:S(2)}) copy-start(bf16[16,1024]{1,0:T(8,128)(2,1)} %tokens.1) | copy-start | bytes 98308
  2.8 0.7 %copy-start.2 = (s32[20,128]{1,0:T(8,128)S(1)}, s32[20,128]{1,0:T(8,128)}, u32[]{:S(2)}) copy-start(s32[20,128]{1,0:T(8,128)} %pvar.1) | copy-start | bytes 30724
  3.5 0.7 %copy-start.3 = (f32[2,1024]{1,0:T(2,128)S(1)}, f32[2,1024]{1,0:T(2,128)}, u32[]{:S(2)}) copy-start(f32[2,1024]{1,0:T(2,128)} %gains.1) | copy-start | bytes 24580
  4.2 0.7 %copy-start.4 = (s32[8,32]{1,0:T(8,128)S(1)}, s32[8,32]{1,0:T(8,128)}, u32[]{:S(2)}) copy-start(s32[8,32]{1,0:T(8,128)} %ptab.1) | copy-start | bytes 3076
  4.9 0.7 %copy-start.5 = (s32[512]{0:T(512)S(1)}, s32[512]{0:T(512)}, u32[]{:S(2)}) copy-start(s32[512]{0:T(512)} %param.23) | copy-start | bytes 6148
  5.6 0.7 %copy-start.6 = (f32[2,16]{1,0:T(2,128)S(1)}, f32[2,16]{1,0:T(2,128)}, u32[]{:S(2)}) copy-start(f32[2,16]{1,0:T(2,128)} %vbias.1) | copy-start | bytes 388
  6.3 0.7 %copy-start.7 = (s32[8]{0:T(128)S(1)}, s32[8]{0:T(128)}, u32[]{:S(2)}) copy-start(s32[8]{0:T(128)} %clen.1) | copy-start | bytes 100
  6.9 0.7 %copy-start.8 = (s32[1,64]{1,0:T(1,128)S(1)}, s32[1,64]{1,0:T(1,128)}, u32[]{:S(2)}) copy-start(s32[1,64]{1,0:T(1,128)} %parents.1) | copy-start | bytes 772
  7.6 0.7 %copy-start.9 = (s32[1,8]{1,0:T(1,128)S(1)}, s32[1,8]{1,0:T(1,128)}, u32[]{:S(2)}) copy-start(s32[1,8]{1,0:T(1,128)} %accepted.1) | copy-start | bytes 100

commit v2 on v1

--- a/solution.py
+++ b/solution.py
@@ -32,11 +32,13 @@
 
 def kernel(
     R, H,
-    tokens, gains, qkv_hbm, out_hbm, gu_hbm, down_hbm, vbias, cache_hbm, pvar, tvar, clen, ptab, parents, accepted,
+    tokens, gains_hbm, qkv_hbm, out_hbm, gu_hbm, down_hbm, vbias_hbm, cache_hbm, pvar_hbm, tvar_hbm, clen_hbm,
+    ptab_hbm, parents_hbm, accepted_hbm,
     mixed, attended, new_kv,
-    qkv, outw, gu, downw, pages, tbuf, qbuf, tvoh, bmat, oh, own_s, fill_s, own_rows, pm, plt, po,
+    gains, vbias, pvar, tvar, clen, ptab, parents, accepted, vt,
+    qkv, outw, gu, downw, pages, tbuf, qbuf, tvoh, bmat, oh, own_s, own_rows, pm, plt, po,
     osend, ssend, obuf, sbuf, gbuf, act, hid, dsend, dbuf,
-    lsem, ts, tr, qs, qr, os_, or_, ss, sr, gs, gr, ds_, dr,
+    lsem, ksem, ts, tr, qs, qr, fs, fr, os_, or_, ss, sr, gs, gr, ds_, dr,
 ):
     req = lax.axis_index("req")
     head = lax.axis_index("head")
@@ -68,6 +70,15 @@
     def _(d):
         pl.semaphore_signal(barrier, inc=1, device_id=at_req(d), device_id_type=pl.DeviceIdType.MESH)
 
+    small = [
+        pltpu.make_async_copy(src, dst, ksem.at[k])
+        for k, (src, dst) in enumerate((
+            (ptab_hbm, ptab), (pvar_hbm, pvar), (clen_hbm, clen), (tvar_hbm, tvar), (vbias_hbm, vbias),
+            (parents_hbm, parents), (accepted_hbm, accepted), (gains_hbm, gains),
+        ))
+    ]
+    for copy in small:
+        copy.start()
     own_tokens = pltpu.make_async_copy(tokens, tbuf.at[head], lsem.at[0])
     own_tokens.start()
     get_qkv = pltpu.make_async_copy(qkv_hbm, qkv, lsem.at[1])
@@ -88,6 +99,8 @@
     for copy in token_copies:
         copy.start()
 
+    for copy in small:
+        copy.wait()
     table = ptab[...]
     place = iota(table.shape, 0) * maxp + iota(table.shape, 1) + 1
     row16 = iota((BROWS, page), 0)
@@ -96,20 +109,56 @@
     pm[...] = jnp.zeros(pm.shape, f32)
     plt[...] = jnp.zeros(plt.shape, f32)
 
-    @pl.loop(0, pool)
-    def _(p):
-        code = jnp.max(jnp.where(table == req * pool + p, place, 0))
-        used = code > 0
-        slot = jnp.maximum(code - 1, 0)
-        owner = slot // maxp
-        filled = jnp.where(used, jnp.clip(clen[owner] - (slot - owner * maxp) * page, 0, page), 0)
-        own_s[p] = owner
-        fill_s[p] = filled
-        own_rows[pl.ds(p, 1), :] = jnp.full((1, C), jnp.where(used, owner, -1), jnp.int32)
-        line = pvar[pl.ds(p, 1), :]
-        hot = jnp.where(row16 < TERMS * NVAR, (line == row16 % NVAR).astype(f32), 0.0)
-        hot = jnp.where(row16 == TERMS * NVAR, (lane16 >= filled).astype(f32), hot)
-        oh[p] = hot.astype(bf16)
+    group = 4 if pool % 4 == 0 else 1
+
+    @pl.loop(0, pool // group)
+    def _(g):
+        for k in range(group):
+            p = g * group + k
+            code = jnp.max(jnp.where(table == req * pool + p, place, 0))
+            used = code > 0
+            slot = jnp.maximum(code - 1, 0)
+            owner = slot // maxp
+            filled = jnp.where(used, jnp.clip(clen[owner] - (slot - owner * maxp) * page, 0, page), 0)
+            own_s[p] = owner
+            own_rows[pl.ds(p, 1), :] = jnp.full((1, C), jnp.where(used, owner, -1), jnp.int32)
+            line = pvar[pl.ds(p, 1), :]
+            hot = jnp.where(row16 < TERMS * NVAR, (line == row16 % NVAR).astype(f32), 0.0)
+            hot = jnp.where(row16 == TERMS * NVAR, (lane16 >= filled).astype(f32), hot)
+            oh[p] = hot.astype(bf16)
+
+    own_tokens.wait()
+    for copy in token_copies:
+        copy.wait()
+    get_qkv.wait()
+    values = tbuf[...].astype(f32).reshape(H * rows, D)
+    normed = rms_scaled(values, gains[0:1, :]).astype(bf16)
+    scale = 1.0 / math.sqrt(HD)
+    query = (dot(normed, qkv[0]).astype(bf16).astype(f32) * scale).astype(bf16)
+    qbuf[req] = query
+
+    half = R // 2
+    partner = req + 1 - 2 * lax.rem(req, 2)
+    beside = {"req": partner, "head": head}
+
+    def query_copy(k):
+        return remote(qbuf.at[req], qbuf.at[req], qs.at[k], qr.at[k], at_req(2 * k))
+
+    def forward_copy(k):
+        source = lax.rem(req + R - 2 * k, R)
+        return remote(qbuf.at[source], qbuf.at[source], fs.at[k], fr.at[k], beside)
+
+    @pl.loop(1, half)
+    def _(k):
+        query_copy(k).start()
+
+    forward_copy(0).start()
+
+    keys = dot(normed, qkv[1]).astype(bf16)
+    vals = dot(normed, qkv[2]).astype(bf16)
+    chosen = (iota((tree, accepted.shape[1]), 0) == accepted[...]).astype(f32).astype(bf16)
+    new_kv[0, 0] = dot(chosen, keys, 0, 0).astype(bf16)
+    new_kv[1, 0] = dot(chosen, vals, 0, 0).astype(bf16)
 
     lane_head = iota((1, C), 1) // tree
     same_row = jnp.zeros((1, C), f32)
@@ -149,28 +198,10 @@
 
     block = (iota((C, QL), 0) // tree == iota((C, QL), 1) // HD).astype(f32).astype(bf16)
 
-    own_tokens.wait()
-    for copy in token_copies:
-        copy.wait()
-    get_qkv.wait()
-    values = tbuf[...].astype(f32).reshape(H * rows, D)
-    normed = rms_scaled(values, gains[0:1, :]).astype(bf16)
-    scale = 1.0 / math.sqrt(HD)
-    query = (dot(normed, qkv[0]).astype(bf16).astype(f32) * scale).astype(bf16)
-    qbuf[req] = query
-
-    def query_copy(d):
-        return remote(qbuf.at[req], qbuf.at[req], qs.at[d], qr.at[d], at_req(d))
-
-    @pl.loop(1, R)
-    def _(d):
-        query_copy(d).start()
-
-    keys = dot(normed, qkv[1]).astype(bf16)
-    vals = dot(normed, qkv[2]).astype(bf16)
-    chosen = (iota((tree, accepted.shape[1]), 0) == accepted[...]).astype(f32).astype(bf16)
-    new_kv[0, 0] = dot(chosen, keys, 0, 0).astype(bf16)
-    new_kv[1, 0] = dot(chosen, vals, 0, 0).astype(bf16)
+    @pl.loop(1, half)
+    def _(k):
+        query_copy(k).wait()
+        forward_copy(k).start()
 
     def spread_query(q):
         return jnp.concatenate([q] * HL, axis=0) * block
@@ -191,11 +222,14 @@
 
     get_pages.wait()
 
-    @pl.loop(1, R)
-    def _(d):
-        query_copy(d).wait()
-
-    group = 4 if pool % 4 == 0 else 1
+    @pl.loop(0, pool // group)
+    def _(g):
+        for k in range(group):
+            vt[g * group + k] = pages[1, g * group + k].T
+
+    @pl.loop(0, half)
+    def _(k):
+        forward_copy(k).wait()
 
     @pl.loop(0, pool // group)
     def _(g):
@@ -207,7 +241,7 @@
             w = jnp.exp(scores - top).astype(bf16)
             pm[pl.ds(p, 1), :] = top
             plt[pl.ds(p, 1), :] = jnp.sum(w.astype(f32), axis=0, keepdims=True)
-            po[p] = pick(dot(pages[1, p], w, 0, 0))
+            po[p] = pick(dot(vt[p], w))
 
     def out_copy(d):
         return remote(osend.at[d], obuf.at[d], os_.at[d], or_.at[d], at_req(d))
@@ -304,6 +338,17 @@
     mixed[...] = (hid[head] + result).astype(bf16)
 
 
+def hand_over(mixed, attended, new_kv, mixed_out, attended_out, new_kv_out, sem):
+    copies = [
+        pltpu.make_async_copy(src, dst, sem.at[k])
+        for k, (src, dst) in enumerate(((mixed, mixed_out), (attended, attended_out), (new_kv, new_kv_out)))
+    ]
+    for copy in copies:
+        copy.start()
+    for copy in copies:
+        copy.wait()
+
+
 def shards(
     tokens, gains, qkv_weight, out_weight, gate_up_weight, down_weight, variate_bias, page_cache, page_variates,
     token_variates, cache_len, page_table, parents, accepted,
@@ -319,18 +364,26 @@
     padded = (pool + 7) // 8 * 8
     hbm = pl.BlockSpec(memory_space=pl.ANY)
     vmem = pl.BlockSpec(memory_space=pltpu.VMEM)
-    smem = pl.BlockSpec(memory_space=pltpu.SMEM)
     dma = pltpu.SemaphoreType.DMA
-    return tuple(pl.pallas_call(
+    results = pl.pallas_call(
         functools.partial(kernel, R, H),
         out_shape=(
             jax.ShapeDtypeStruct((rows, D), bf16),
             jax.ShapeDtypeStruct((tree, QL), bf16),
             jax.ShapeDtypeStruct((2, 1, accepted.shape[1], QL), bf16),
         ),
-        in_specs=[hbm, vmem, hbm, hbm, hbm, hbm, smem, hbm, vmem, vmem, smem, vmem, vmem, vmem],
+        in_specs=[hbm] * 14,
         out_specs=(vmem, vmem, vmem),
         scratch_shapes=[
+            pltpu.VMEM(gains.shape, f32),
+            pltpu.SMEM(variate_bias.shape, f32),
+            pltpu.VMEM(page_variates.shape, jnp.int32),
+            pltpu.VMEM((1, token_variates.shape[0]), jnp.int32),
+            pltpu.SMEM(cache_len.shape, jnp.int32),
+            pltpu.VMEM(page_table.shape, jnp.int32),
+            pltpu.VMEM(parents.shape, jnp.int32),
+            pltpu.VMEM(accepted.shape, jnp.int32),
+            pltpu.VMEM((pool, QL, page), bf16),
             pltpu.VMEM(qkv_weight.shape, bf16),
             pltpu.VMEM(out_weight.shape, bf16),
             pltpu.VMEM(gate_up_weight.shape, bf16),
@@ -341,7 +394,6 @@
             pltpu.VMEM((R, BROWS, tree), bf16),
             pltpu.VMEM((R, BROWS, C), bf16),
             pltpu.VMEM((pool, BROWS, page), bf16),
-            pltpu.SMEM((pool,), jnp.int32),
             pltpu.SMEM((pool,), jnp.int32),
             pltpu.VMEM((padded, C), jnp.int32),
             pltpu.VMEM((padded, C), f32),
@@ -357,7 +409,9 @@
             pltpu.VMEM((H, rows, D), bf16),
             pltpu.VMEM((H, rows, D), bf16),
             dma((6,)),
+            dma((8,)),
             dma((H,)), dma((H,)),
+            dma((R,)), dma((R,)),
             dma((R,)), dma((R,)),
             dma((R,)), dma((R,)),
             dma((R,)), dma((R,)),
@@ -365,13 +419,21 @@
             dma((H,)), dma((H,)),
         ],
         compiler_params=pltpu.CompilerParams(
-            collective_id=0, has_side_effects=True, vmem_limit_bytes=52 * 1024 * 1024
+            collective_id=0, has_side_effects=True, vmem_limit_bytes=60 * 1024 * 1024
         ),
         cost_estimate=pl.CostEstimate(flops=10**9, bytes_accessed=12 * 10**6, transcendentals=10**6),
     )(
         tokens, gains, qkv_weight, out_weight, gate_up_weight, down_weight, variate_bias, page_cache, page_variates,
         token_variates.reshape(1, -1), cache_len, page_table, parents, accepted,
-    ))
+    )
+    return tuple(pl.pallas_call(
+        hand_over,
+        out_shape=tuple(jax.ShapeDtypeStruct(a.shape, a.dtype) for a in results),
+        in_specs=[hbm] * 3,
+        out_specs=(hbm,) * 3,
+        scratch_shapes=[dma((3,))],
+        compiler_params=pltpu.CompilerParams(vmem_limit_bytes=60 * 1024 * 1024),
+    )(*results))
 
 
 def solution(mesh):

time: 51.9 us -> 46 us (0.89)
  local copies, waits for them, and re-layouts: 9.4 us -> 0 us
  Pallas kernels: 41.4 us -> 45.2 us
    unnamed x23 -> x0, local copies, waits for them, and re-layouts: 9.4 us -> none
    pallas_call x0 -> x1, Pallas kernels: none -> 3.36 us  [shards(): pl.pallas_call(hand_over, out_shape=tuple((jax.ShapeDtypeStruct(a.shape,...]
where the time goes in v2:
time: 46 us; the launch traced here: 45.8 us
  Pallas kernels  45.2 us (98%)
  between operations  0.64 us (1%)
    pallas_call x1, Pallas kernels, shards(): pl.pallas_call(functools.partial(kernel, R, H), out_shape=(jax.ShapeDtype...  41.8 us
    pallas_call x1, Pallas kernels, shards(): pl.pallas_call(hand_over, out_shape=tuple((jax.ShapeDtypeStruct(a.shape,...  3.36 us

profile of v2, /device:TPU:0, one launch (start us, length us, event | category | flops | bytes accessed | tf_op | source)
XLA Modules:
  0.0 45.8 jit_solution(10866089194374485865)
XLA Ops:
  0.6 41.8 %shard_map.157 = (bf16[16,1024]{1,0:T(8,128)(2,1)}, bf16[64,256]{1,0:T(8,128)(2,1)}, bf16[2,1,8,256]{3,2,1,0:T(8,128)(2,1)}) custom-call(bf16[16,1024]{1,0:T(8,128)(2,1)} %tokens.1, f32[2,1024]{1,0:T(2,128)} %gains_hbm.1, bf16[3,1024,256]{2,1,0:T(8,128)(2,1)} %qkv_hbm.1, bf16[1024,1024]{1,0:T(8,128)(2,1)} %out_hbm.1, bf16[2,1024,1024]{2,1,0:T(8,128)(2,1)} %gu_hbm.1, ...), custom_call_target="tpu_custom_call" | custom-call | flops 1000000000 | bytes 12000000 | tf_op jit(solution)/shard_map/pallas_call | solution.py:368
  42.4 3.4 %shard_map.158 = (bf16[16,1024]{1,0:T(8,128)(2,1)}, bf16[64,256]{1,0:T(8,128)(2,1)}, bf16[2,1,8,256]{3,2,1,0:T(8,128)(2,1)}) custom-call(bf16[16,1024]{1,0:T(8,128)(2,1)} %get-tuple-element.6.mixed, bf16[64,256]{1,0:T(8,128)(2,1)} %get-tuple-element.7.attended, bf16[2,1,8,256]{3,2,1,0:T(8,128)(2,1)} %get-tuple-element.8.new_kv), custom_call_target="tpu_custom_call" | custom-call | tf_op jit(solution)/shard_map/pallas_call | solution.py:429

commit v3 on v2

--- a/solution.py
+++ b/solution.py
@@ -12,6 +12,7 @@
 NVAR = 4
 TERMS = 3
 BROWS = 16
+STEP = 256
 epsilon = 1e-06
 low = -1e30
 f32 = jnp.float32
@@ -160,6 +161,11 @@
     new_kv[0, 0] = dot(chosen, keys, 0, 0).astype(bf16)
     new_kv[1, 0] = dot(chosen, vals, 0, 0).astype(bf16)
 
+    @pl.loop(1, half)
+    def _(k):
+        query_copy(k).wait()
+        forward_copy(k).start()
+
     lane_head = iota((1, C), 1) // tree
     same_row = jnp.zeros((1, C), f32)
     other_row = jnp.zeros((1, C), f32)
@@ -198,11 +204,6 @@
 
     block = (iota((C, QL), 0) // tree == iota((C, QL), 1) // HD).astype(f32).astype(bf16)
 
-    @pl.loop(1, half)
-    def _(k):
-        query_copy(k).wait()
-        forward_copy(k).start()
-
     def spread_query(q):
         return jnp.concatenate([q] * HL, axis=0) * block
 
@@ -260,13 +261,11 @@
             out = out + factor[p : p + 1] * po[p]
         return top, total, out
 
-    srow = iota((8, C), 0)
-
     @pl.loop(1, R)
     def _(d):
         top, total, out = merged(lax.rem(req + d, R))
         osend[d] = out.astype(bf16)
-        ssend[d] = jnp.where(srow == 0, top, total)
+        ssend[d] = jnp.concatenate([top, total], axis=0)
         out_copy(d).start()
         stat_copy(d).start()
 
@@ -274,7 +273,6 @@
     new_top = jnp.maximum(top, tree_max)
     fa = jnp.exp(top - new_top)
     fb = jnp.exp(tree_max - new_top)
-    osend[0] = jnp.zeros((HD, C), bf16)
     total = total * fa + tree_total * fb
     out = out * fa + tree_out * fb
     top = new_top
@@ -315,37 +313,48 @@
     hid[...] = state.reshape(H, rows, D)
     normed_two = rms_scaled(state, gains[1:2, :]).astype(bf16)
     get_gu.wait()
-    step = 256
+    step = STEP
     for c in range(0, FFL, step):
         gate = dot(normed_two, gu[0, :, c : c + step])
         upward = dot(normed_two, gu[1, :, c : c + step])
         act[:, c : c + step] = (gate / (1.0 + jnp.exp(-gate)) * upward).astype(bf16)
     get_down.wait()
     activated = act[...]
-    for c in range(0, D, step):
-        part = dot(activated, downw[:, c : c + step])
-        dsend[:, :, c : c + step] = part.reshape(H, rows, step).astype(bf16)
-    down_copies = [
-        remote(dsend.at[lax.rem(head + d, H)], dbuf.at[d - 1], ds_.at[d - 1], dr.at[d - 1], at_head(d))
-        for d in range(1, H)
-    ]
-    for copy in down_copies:
-        copy.start()
+    def down_copy(d, n):
+        columns = pl.ds(n * step, step)
+        return remote(
+            dsend.at[lax.rem(head + d, H), :, columns], dbuf.at[d - 1, :, columns],
+            ds_.at[d - 1, n], dr.at[d - 1, n], at_head(d),
+        )
+
+    for n in range(D // step):
+        part = dot(activated, downw[:, n * step : (n + 1) * step])
+        dsend[:, :, n * step : (n + 1) * step] = part.reshape(H, rows, step).astype(bf16)
+        for d in range(1, H):
+            down_copy(d, n).start()
     result = dsend[head].astype(f32)
     for d in range(1, H):
-        down_copies[d - 1].wait()
+        for n in range(D // step):
+            down_copy(d, n).wait()
         result = result + dbuf[d - 1].astype(f32)
     mixed[...] = (hid[head] + result).astype(bf16)
 
 
-def hand_over(mixed, attended, new_kv, mixed_out, attended_out, new_kv_out, sem):
-    copies = [
+def hand_over(mixed, attended, new_kv, mixed_out, attended_out, new_kv_out, one, two, three, sem):
+    fetch = [
         pltpu.make_async_copy(src, dst, sem.at[k])
-        for k, (src, dst) in enumerate(((mixed, mixed_out), (attended, attended_out), (new_kv, new_kv_out)))
+        for k, (src, dst) in enumerate(((mixed, one), (attended, two), (new_kv, three)))
     ]
-    for copy in copies:
+    store = [
+        pltpu.make_async_copy(src, dst, sem.at[3 + k])
+        for k, (src, dst) in enumerate(((one, mixed_out), (two, attended_out), (three, new_kv_out)))
+    ]
+    for copy in fetch:
         copy.start()
-    for copy in copies:
+    for k in range(3):
+        fetch[k].wait()
+        store[k].start()
+    for copy in store:
         copy.wait()
 
 
@@ -400,9 +409,9 @@
             pltpu.VMEM((padded, C), f32),
             pltpu.VMEM((pool, HD, C), f32),
             pltpu.VMEM((R, HD, C), bf16),
-            pltpu.VMEM((R, 8, C), f32),
+            pltpu.VMEM((R, 2, C), f32),
             pltpu.VMEM((R, HD, C), bf16),
-            pltpu.VMEM((R, 8, C), f32),
+            pltpu.VMEM((R, 2, C), f32),
             pltpu.VMEM((H, tree, QL), bf16),
             pltpu.VMEM((tree, gate_up_weight.shape[2]), bf16),
             pltpu.VMEM((H, rows, D), f32),
@@ -416,7 +425,7 @@
             dma((R,)), dma((R,)),
             dma((R,)), dma((R,)),
             dma((H,)), dma((H,)),
-            dma((H,)), dma((H,)),
+            dma((H, D // STEP)), dma((H, D // STEP)),
         ],
         compiler_params=pltpu.CompilerParams(
             collective_id=0, has_side_effects=True, vmem_limit_bytes=60 * 1024 * 1024
@@ -431,7 +440,7 @@
         out_shape=tuple(jax.ShapeDtypeStruct(a.shape, a.dtype) for a in results),
         in_specs=[hbm] * 3,
         out_specs=(hbm,) * 3,
-        scratch_shapes=[dma((3,))],
+        scratch_shapes=[pltpu.VMEM(a.shape, a.dtype) for a in results] + [dma((6,))],
         compiler_params=pltpu.CompilerParams(vmem_limit_bytes=60 * 1024 * 1024),
     )(*results))
 

time: 46 us -> 42.7 us (0.928)
  Pallas kernels: 45.2 us -> 41.9 us
    pallas_call x1, Pallas kernels: 3.36 us -> 1.44 us  [shards(): pl.pallas_call(hand_over, out_shape=tuple((jax.ShapeDtypeStruct(a.shape,...]
    pallas_call x1, Pallas kernels: 41.8 us -> 40.5 us  [shards(): pl.pallas_call(functools.partial(kernel, R, H), out_shape=(jax.ShapeDtype...]
where the time goes in v3:
time: 42.7 us; the launch traced here: 42.6 us
  Pallas kernels  41.9 us (98%)
  between operations  0.64 us (1%)
    pallas_call x1, Pallas kernels, shards(): pl.pallas_call(functools.partial(kernel, R, H), out_shape=(jax.ShapeDtype...  40.5 us
    pallas_call x1, Pallas kernels, shards(): pl.pallas_call(hand_over, out_shape=tuple((jax.ShapeDtypeStruct(a.shape,...  1.44 us

profile of v3, /device:TPU:0, one launch (start us, length us, event | category | flops | bytes accessed | tf_op | source)
XLA Modules:
  0.0 42.6 jit_solution(18243818978827830050)
XLA Ops:
  0.6 40.5 %shard_map.157 = (bf16[16,1024]{1,0:T(8,128)(2,1)}, bf16[64,256]{1,0:T(8,128)(2,1)}, bf16[2,1,8,256]{3,2,1,0:T(8,128)(2,1)}) custom-call(bf16[16,1024]{1,0:T(8,128)(2,1)} %tokens.1, f32[2,1024]{1,0:T(2,128)} %gains_hbm.1, bf16[3,1024,256]{2,1,0:T(8,128)(2,1)} %qkv_hbm.1, bf16[1024,1024]{1,0:T(8,128)(2,1)} %out_hbm.1, bf16[2,1024,1024]{2,1,0:T(8,128)(2,1)} %gu_hbm.1, ...), custom_call_target="tpu_custom_call" | custom-call | flops 1000000000 | bytes 12000000 | tf_op jit(solution)/shard_map/pallas_call | solution.py:377
  41.1 1.4 %shard_map.158 = (bf16[16,1024]{1,0:T(8,128)(2,1)}, bf16[64,256]{1,0:T(8,128)(2,1)}, bf16[2,1,8,256]{3,2,1,0:T(8,128)(2,1)}) custom-call(bf16[16,1024]{1,0:T(8,128)(2,1)} %get-tuple-element.6.mixed, bf16[64,256]{1,0:T(8,128)(2,1)} %get-tuple-element.7.attended, bf16[2,1,8,256]{3,2,1,0:T(8,128)(2,1)} %get-tuple-element.8.new_kv), custom_call_target="tpu_custom_call" | custom-call | tf_op jit(solution)/shard_map/pallas_call | solution.py:438

commit v4 on v3

--- a/solution.py
+++ b/solution.py
@@ -36,7 +36,7 @@
     tokens, gains_hbm, qkv_hbm, out_hbm, gu_hbm, down_hbm, vbias_hbm, cache_hbm, pvar_hbm, tvar_hbm, clen_hbm,
     ptab_hbm, parents_hbm, accepted_hbm,
     mixed, attended, new_kv,
-    gains, vbias, pvar, tvar, clen, ptab, parents, accepted, vt,
+    gains, vbias, pvar, tvar, clen, ptab, parents, accepted, vt, oht,
     qkv, outw, gu, downw, pages, tbuf, qbuf, tvoh, bmat, oh, own_s, own_rows, pm, plt, po,
     osend, ssend, obuf, sbuf, gbuf, act, hid, dsend, dbuf,
     lsem, ksem, ts, tr, qs, qr, fs, fr, os_, or_, ss, sr, gs, gr, ds_, dr,
@@ -128,6 +128,16 @@
             hot = jnp.where(row16 == TERMS * NVAR, (lane16 >= filled).astype(f32), hot)
             oh[p] = hot.astype(bf16)
 
+    spread = (iota((tree, C), 0) == iota((tree, C), 1) % tree).astype(f32).astype(bf16)
+    block = (iota((QL, C), 0) // HD == iota((QL, C), 1) // tree).astype(f32).astype(bf16)
+    head_lanes = iota((HD, C), 1) // tree
+
+    def pick(wide):
+        out = wide[0:HD]
+        for h in range(1, HL):
+            out = jnp.where(head_lanes == h, wide[h * HD : (h + 1) * HD], out)
+        return out
+
     own_tokens.wait()
     for copy in token_copies:
         copy.wait()
@@ -136,6 +146,7 @@
     normed = rms_scaled(values, gains[0:1, :]).astype(bf16)
     scale = 1.0 / math.sqrt(HD)
     query = (dot(normed, qkv[0]).astype(bf16).astype(f32) * scale).astype(bf16)
+    query = pick(dot(query, spread, 0, 0)).astype(bf16)
     qbuf[req] = query
 
     half = R // 2
@@ -182,7 +193,6 @@
 
     same_terms = split(same_row)
     other_terms = split(other_row)
-    spread = (iota((tree, C), 0) == iota((tree, C), 1) % tree).astype(f32).astype(bf16)
     brow = iota((BROWS, C), 0)
     trow = iota((BROWS, tree), 0)
     for r in range(R):
@@ -202,20 +212,10 @@
     reach8 = clip(dot(reach4, reach4))
     allowed = dot(reach8, spread) > 0.5
 
-    block = (iota((C, QL), 0) // tree == iota((C, QL), 1) // HD).astype(f32).astype(bf16)
-
     def spread_query(q):
         return jnp.concatenate([q] * HL, axis=0) * block
 
-    head_lanes = iota((HD, C), 1) // tree
-
-    def pick(wide):
-        out = wide[0:HD]
-        for h in range(1, HL):
-            out = jnp.where(head_lanes == h, wide[h * HD : (h + 1) * HD], out)
-        return out
-
-    tree_scores = dot(keys, spread_query(query), 1, 1) + dot(tvoh[req], bmat[req], 0, 0)
+    tree_scores = dot(keys, spread_query(query)) + dot(tvoh[req], bmat[req], 0, 0)
     tree_max = jnp.max(jnp.where(allowed, tree_scores, low), axis=0, keepdims=True)
     tree_w = jnp.where(allowed, jnp.exp(tree_scores - tree_max), 0.0).astype(bf16)
     tree_total = jnp.sum(tree_w.astype(f32), axis=0, keepdims=True)
@@ -227,6 +227,7 @@
     def _(g):
         for k in range(group):
             vt[g * group + k] = pages[1, g * group + k].T
+            oht[g * group + k] = oh[g * group + k].T
 
     @pl.loop(0, half)
     def _(k):
@@ -237,7 +238,7 @@
         for k in range(group):
             p = g * group + k
             owner = own_s[p]
-            scores = dot(pages[0, p], spread_query(qbuf[owner]), 1, 1) + dot(oh[p], bmat[owner], 0, 0)
+            scores = dot(pages[0, p], spread_query(qbuf[owner])) + dot(oht[p], bmat[owner])
             top = jnp.max(scores, axis=0, keepdims=True)
             w = jnp.exp(scores - top).astype(bf16)
             pm[pl.ds(p, 1), :] = top
@@ -294,10 +295,7 @@
         total = total + stats[1:2] * fd
         out = out + obuf[d].astype(f32) * fd
     att_t = (out / total).astype(bf16)
-    diag = jnp.concatenate([att_t] * HL, axis=0) * (
-        iota((HL * HD, C), 0) // HD == iota((HL * HD, C), 1) // tree
-    ).astype(f32).astype(bf16)
-    att = dot(spread, diag, 1, 1).astype(bf16)
+    att = dot(spread, spread_query(att_t), 1, 1).astype(bf16)
     gbuf[head] = att
     att_copies = [remote(gbuf.at[head], gbuf.at[head], gs.at[d - 1], gr.at[d - 1], at_head(d)) for d in range(1, H)]
     for copy in att_copies:
@@ -393,13 +391,14 @@
             pltpu.VMEM(parents.shape, jnp.int32),
             pltpu.VMEM(accepted.shape, jnp.int32),
             pltpu.VMEM((pool, QL, page), bf16),
+            pltpu.VMEM((pool, page, BROWS), bf16),
             pltpu.VMEM(qkv_weight.shape, bf16),
             pltpu.VMEM(out_weight.shape, bf16),
             pltpu.VMEM(gate_up_weight.shape, bf16),
             pltpu.VMEM(down_weight.shape, bf16),
             pltpu.VMEM(page_cache.shape, bf16),
             pltpu.VMEM((H, rows, D), bf16),
-            pltpu.VMEM((R, tree, QL), bf16),
+            pltpu.VMEM((R, HD, C), bf16),
             pltpu.VMEM((R, BROWS, tree), bf16),
             pltpu.VMEM((R, BROWS, C), bf16),
             pltpu.VMEM((pool, BROWS, page), bf16),

time: 42.7 us -> 39.6 us (0.927)
  Pallas kernels: 41.9 us -> 38.8 us
    pallas_call x1, Pallas kernels: 40.5 us -> 37.3 us  [shards(): pl.pallas_call(functools.partial(kernel, R, H), out_shape=(jax.ShapeDtype...]
where the time goes in v4:
time: 39.6 us; the launch traced here: 39.4 us
  Pallas kernels  38.8 us (98%)
  between operations  0.64 us (2%)
    pallas_call x1, Pallas kernels, shards(): pl.pallas_call(functools.partial(kernel, R, H), out_shape=(jax.ShapeDtype...  37.3 us
    pallas_call x1, Pallas kernels, shards(): pl.pallas_call(hand_over, out_shape=tuple((jax.ShapeDtypeStruct(a.shape,...  1.44 us

profile of v4, /device:TPU:0, one launch (start us, length us, event | category | flops | bytes accessed | tf_op | source)
XLA Modules:
  0.0 39.4 jit_solution(8666518269472368135)
XLA Ops:
  0.6 37.3 %shard_map.157 = (bf16[16,1024]{1,0:T(8,128)(2,1)}, bf16[64,256]{1,0:T(8,128)(2,1)}, bf16[2,1,8,256]{3,2,1,0:T(8,128)(2,1)}) custom-call(bf16[16,1024]{1,0:T(8,128)(2,1)} %tokens.1, f32[2,1024]{1,0:T(2,128)} %gains_hbm.1, bf16[3,1024,256]{2,1,0:T(8,128)(2,1)} %qkv_hbm.1, bf16[1024,1024]{1,0:T(8,128)(2,1)} %out_hbm.1, bf16[2,1024,1024]{2,1,0:T(8,128)(2,1)} %gu_hbm.1, ...), custom_call_target="tpu_custom_call" | custom-call | flops 1000000000 | bytes 12000000 | tf_op jit(solution)/shard_map/pallas_call | solution.py:375
  38.0 1.4 %shard_map.158 = (bf16[16,1024]{1,0:T(8,128)(2,1)}, bf16[64,256]{1,0:T(8,128)(2,1)}, bf16[2,1,8,256]{3,2,1,0:T(8,128)(2,1)}) custom-call(bf16[16,1024]{1,0:T(8,128)(2,1)} %get-tuple-element.6.mixed, bf16[64,256]{1,0:T(8,128)(2,1)} %get-tuple-element.7.attended, bf16[2,1,8,256]{3,2,1,0:T(8,128)(2,1)} %get-tuple-element.8.new_kv), custom_call_target="tpu_custom_call" | custom-call | tf_op jit(solution)/shard_map/pallas_call | solution.py:437

commit v5 on v4

--- a/solution.py
+++ b/solution.py
@@ -233,10 +233,12 @@
     def _(k):
         forward_copy(k).wait()
 
-    @pl.loop(0, pool // group)
+    wide = 10 if pool % 10 == 0 else 1
+
+    @pl.loop(0, pool // wide)
     def _(g):
-        for k in range(group):
-            p = g * group + k
+        for k in range(wide):
+            p = g * wide + k
             owner = own_s[p]
             scores = dot(pages[0, p], spread_query(qbuf[owner])) + dot(oht[p], bmat[owner])
             top = jnp.max(scores, axis=0, keepdims=True)

time: 39.6 us -> 38.1 us (0.962)
  Pallas kernels: 38.8 us -> 37.2 us
    pallas_call x1, Pallas kernels: 37.3 us -> 35.8 us  [shards(): pl.pallas_call(functools.partial(kernel, R, H), out_shape=(jax.ShapeDtype...]
where the time goes in v5:
time: 38.1 us; the launch traced here: 37.9 us
  Pallas kernels  37.2 us (98%)
  between operations  0.64 us (2%)
    pallas_call x1, Pallas kernels, shards(): pl.pallas_call(functools.partial(kernel, R, H), out_shape=(jax.ShapeDtype...  35.8 us
    pallas_call x1, Pallas kernels, shards(): pl.pallas_call(hand_over, out_shape=tuple((jax.ShapeDtypeStruct(a.shape,...  1.44 us

profile of v5, /device:TPU:0, one launch (start us, length us, event | category | flops | bytes accessed | tf_op | source)
XLA Modules:
  0.0 37.9 jit_solution(13102202786640550276)
XLA Ops:
  0.6 35.8 %shard_map.157 = (bf16[16,1024]{1,0:T(8,128)(2,1)}, bf16[64,256]{1,0:T(8,128)(2,1)}, bf16[2,1,8,256]{3,2,1,0:T(8,128)(2,1)}) custom-call(bf16[16,1024]{1,0:T(8,128)(2,1)} %tokens.1, f32[2,1024]{1,0:T(2,128)} %gains_hbm.1, bf16[3,1024,256]{2,1,0:T(8,128)(2,1)} %qkv_hbm.1, bf16[1024,1024]{1,0:T(8,128)(2,1)} %out_hbm.1, bf16[2,1024,1024]{2,1,0:T(8,128)(2,1)} %gu_hbm.1, ...), custom_call_target="tpu_custom_call" | custom-call | flops 1000000000 | bytes 12000000 | tf_op jit(solution)/shard_map/pallas_call | solution.py:377
  36.4 1.4 %shard_map.158 = (bf16[16,1024]{1,0:T(8,128)(2,1)}, bf16[64,256]{1,0:T(8,128)(2,1)}, bf16[2,1,8,256]{3,2,1,0:T(8,128)(2,1)}) custom-call(bf16[16,1024]{1,0:T(8,128)(2,1)} %get-tuple-element.6.mixed, bf16[64,256]{1,0:T(8,128)(2,1)} %get-tuple-element.7.attended, bf16[2,1,8,256]{3,2,1,0:T(8,128)(2,1)} %get-tuple-element.8.new_kv), custom_call_target="tpu_custom_call" | custom-call | tf_op jit(solution)/shard_map/pallas_call | solution.py:439
